TPU v7x, 32 devices: a whole 2x2x4 slice. The times are simulated.
32 devices in a mesh: row: 4 (over y, x), col: 8 (over z, core).
Axes of the slice: x: 2, y: 2, z: 4, core: 2. Of those that a mesh axis runs over, the one named last changes fastest.
Arguments:
- traces: bfloat16 [64, 4096], P(None, ('row', 'col')), may hold values from -6 to 6
- incident: bfloat16 [64, 4096], P(None, ('row', 'col')), may hold values from -6 to 6
- points: float32 [3, 4096], P(None, ('row', 'col')), may hold values from 0 to 1
- coupling: int32 [4096], P(('row', 'col')), may hold values from 0 to 2047, as said below
- volume_tiles: bfloat16 [16, 32, 4, 128, 128], P('row', 'col'), may hold values from -0.125 to 0.125
- tile_columns: int32 [16, 32, 4], P('row', 'col'), may hold values from 0 to 8, as said below
Outputs:
- traces_out: bfloat16 [64, 4096], P(None, ('row', 'col'))
- volume_out: float32 [64, 16, 32, 128], P(None, 'row', 'col')
Inputs may be any that keep to these rules, and one draw needn't show every extreme that they name: `coupling`: within each aligned block of 128 unknowns the values are distinct. `tile_columns`: the 4 entries of one tile are distinct, and one of them is 4.
All inputs are finite; a program needn't handle non-finite values.
Results may differ from a plain program's by a relative error of at most 0.0154.
Values may be sent and summed in bfloat16 or wider, within the bound.
A program may use at most 64 MiB of HBM per device.

v0:
```python
import math

import jax
import jax.numpy as jnp
from jax import lax
from jax.sharding import PartitionSpec as P

OUTER_STEPS = 2
PASSES = 2


def with_halo(value, sides, width):
    for axis, dim in sides:
        size, length = (lax.axis_size(axis), value.shape[dim])
        up = [(i, (i + 1) % size) for i in range(size - 1)]
        down = [(j, i) for i, j in up]
        last = lax.slice_in_dim(value, length - width, length, axis=dim)
        initial = lax.slice_in_dim(value, 0, width, axis=dim)
        before = lax.ppermute(last, axis, up)
        after = lax.ppermute(initial, axis, down)
        value = jnp.concatenate([before, value, after], axis=dim)
    return value


def wave_constants(total):
    spacing = float(total) ** (-1.0 / 3.0)
    return (2.0 / spacing, (0.5 * spacing) ** 2, 1.0 / math.sqrt(2.0 * total))


def kernel_block(source_points, target_points, consts):
    wave, smooth, factor = consts
    delta_x = source_points[0][:, None] - target_points[0][None, :]
    delta_y = source_points[1][:, None] - target_points[1][None, :]
    delta_z = source_points[2][:, None] - target_points[2][None, :]
    radius = jnp.sqrt(delta_x * delta_x + delta_y * delta_y + delta_z * delta_z + smooth)
    return (factor * jnp.cos(wave * radius) / radius).astype(jnp.bfloat16)


def block_length(total, limit):
    for candidate in range(min(total, limit), 0, -1):
        if total % candidate == 0:
            return candidate
    return 1


def make_accumulator(source_points, target_points, consts):
    target_total = target_points.shape[1]

    def accumulate(totals, piece, start):
        width = piece.shape[1]
        span = block_length(target_total, max(1, 2**21 // width))

        def add_block(number, running):
            begin = number * span
            targets = lax.dynamic_slice_in_dim(target_points, begin, span, 1)
            kernel = kernel_block(source_points, targets, consts)
            update = jnp.dot(piece, kernel, preferred_element_type=jnp.float32)
            before = lax.dynamic_slice_in_dim(running, begin, span, 1)
            return lax.dynamic_update_slice_in_dim(running, before + update, begin, 1)

        return lax.fori_loop(0, target_total // span, add_block, totals)

    return accumulate


def apply_tiles(rounded, volume_tiles, masks):
    tiles_y, tiles_x, tile_count, tile_side, _ = volume_tiles.shape
    padded = with_halo(rounded, (("row", 1), ("col", 2)), 1)
    picked = jnp.zeros(rounded.shape[:3] + (tile_count, tile_side), jnp.bfloat16)
    for offset in range(9):
        first = offset // 3
        second = offset % 3
        view = padded[:, first : first + tiles_y, second : second + tiles_x, :]
        picked = jnp.where(masks[offset][None, :, :, :, None], view[:, :, :, None, :], picked)
    return jnp.einsum("eyxkq,yxkpq->eyxp", picked, volume_tiles, preferred_element_type=jnp.float32)


def per_device(traces, incident, points, coupling, volume_tiles, tile_columns):
    excitations, shard_len = traces.shape
    row_count = lax.axis_size("row")
    column_count = lax.axis_size("col")
    total = shard_len * row_count * column_count
    consts = wave_constants(total)
    along_row = lax.all_gather(points, "row", axis=1, tiled=True)
    along_col = lax.all_gather(points, "col", axis=1, tiled=True)
    tiles_y, tiles_x, tile_count, tile_side, _ = volume_tiles.shape
    vol_rows = tiles_y * tiles_x * tile_side
    masks = [tile_columns == offset for offset in range(9)]
    present = traces
    field = jnp.zeros((excitations, tiles_y, tiles_x, tile_side), jnp.float32)
    for outer in range(OUTER_STEPS):
        accumulate = make_accumulator(along_row, along_col, consts)
        empty = jnp.zeros((excitations, column_count * shard_len), jnp.float32)
        partial_sums = accumulate(
            empty, lax.all_gather(present, "row", axis=1, tiled=True), jnp.int32(0)
        )
        currents = lax.psum_scatter(
            partial_sums.astype(jnp.bfloat16), "col", scatter_dimension=1, tiled=True
        ).astype(jnp.float32)
        source = jnp.zeros((excitations, vol_rows), jnp.float32).at[:, coupling].set(currents)
        source = source.reshape(excitations, tiles_y, tiles_x, tile_side)
        field = source
        for sweep in range(PASSES):
            rounded = field.astype(jnp.bfloat16)
            field = source + apply_tiles(rounded, volume_tiles, masks)
        readout = jnp.take(field.reshape(excitations, vol_rows), coupling, axis=1)
        present = (incident.astype(jnp.float32) + readout).astype(jnp.bfloat16)
    return (present, field)


def solution(mesh):
    in_specs = (
        P(None, ("row", "col")),
        P(None, ("row", "col")),
        P(None, ("row", "col")),
        P(("row", "col")),
        P("row", "col", None, None, None),
        P("row", "col", None),
    )
    out_specs = (P(None, ("row", "col")), P(None, "row", "col", None))
    return jax.shard_map(
        per_device, mesh=mesh, in_specs=in_specs, out_specs=out_specs, check_vma=False
    )
```

profile of v0, /device:TPU:3, one launch (start us, length us, event | category | flops | bytes accessed | tf_op | source)
XLA Modules:
  0.0 226.9 jit_solution(4217727695652889160)
XLA Ops:
  7.2 13.7 %all_gather.13 = f32[3,1024]{1,0:T(4,128)S(1)} all-gather(f32[3,128]{1,0:T(4,128)} %param.10), channel_id=1, replica_groups=mesh['row'=4,'col'=8] {'col'}, dimensions={1}, use_global_device_ids=true | all-gather | bytes 13824 | tf_op jit(solution)/shard_map/all_gather | solution.py:85
  20.9 6.0 %all_gather.12 = f32[3,512]{1,0:T(4,128)S(1)} all-gather(f32[3,128]{1,0:T(4,128)} %param.10), channel_id=1, replica_groups=mesh['row'=4,'col'=8] {'row'}, dimensions={1}, use_global_device_ids=true | all-gather | bytes 7680 | tf_op jit(solution)/shard_map/all_gather | solution.py:84
  26.9 5.6 %all_gather.14 = bf16[64,512]{1,0:T(8,128)(2,1)S(1)} all-gather(bf16[64,128]{1,0:T(8,128)(2,1)} %param.8), channel_id=1, replica_groups=mesh['row'=4,'col'=8] {'row'}, dimensions={1}, use_global_device_ids=true | all-gather | bytes 81920 | tf_op jit(solution)/shard_map/all_gather | solution.py:95
  33.3 8.3 %fusion.6 = bf16[64,1024]{1,0:T(8,128)(2,1)S(1)} fusion(bf16[64,512]{1,0:T(8,128)(2,1)S(1)} %all_gather.14, f32[1024]{0:T(1024)S(1)} %bitcast.74, f32[512]{0:T(512)S(1)} %bitcast.80, f32[1024]{0:T(1024)S(1)} %bitcast.76, f32[512]{0:T(512)S(1)} %bitcast.82, f32[1024]{0:T(1024)S(1)} %bitcast.72, f32[512]{0:T(512)S(1)} %bitcast.78), kind=kOutput, calls=%fused_computation.17 | convolution fusion | flops 73990144 | bytes 215040 | tf_op jit(solution)/shard_map/while/body/eval_jaxpr/dot_general | solution.py:57
  41.6 0.8 copy.91
  43.2 29.4 %reduce-scatter.7.cloned.1.call-done = bf16[128,64]{1,0:T(8,128)(2,1)} async-done(((bf16[1024,64]{1,0:T(8,128)(2,1)}), bf16[128,64]{1,0:T(8,128)(2,1)}) %reduce-scatter.7.cloned.1.call-update) | async-done | bytes 16400
  72.6 0.8 copy.92
  73.6 1.1 scatter_custom_fusion
  75.8 2.0 collective-permute-start.1
  77.8 4.2 %collective-permute-start = (bf16[64,1,4,128]{3,2,1,0:T(4,128)(2,1)}, bf16[64,1,4,128]{3,2,1,0:T(4,128)(2,1)S(1)}, u32[]{:S(2)}, u32[]{:S(2)}) collective-permute-start(bf16[64,1,4,128]{3,2,1,0:T(4,128)(2,1)} %get-tuple-element.99), channel_id=1, source_target_pairs={{0,8},{8,16},{16,24},{1,9},{9,17},{17,25},{2,10},{10,18},{18,26},{... | collective-permute-start | bytes 196616 | tf_op jit(solution)/shard_map/ppermute | solution.py:19
  82.0 1.3 compare_and_fusion
  84.0 1.1 copy.59
  85.8 6.3 %collective-permute-start.2 = (bf16[64,6,1,128]{3,2,1,0:T(2,128)(2,1)S(1)}, bf16[64,6,1,128]{3,2,1,0:T(2,128)(2,1)S(1)}, u32[]{:S(2)}, u32[]{:S(2)}) collective-permute-start(bf16[64,6,1,128]{3,2,1,0:T(2,128)(2,1)S(1)} %get-tuple-element.83), channel_id=1, source_target_pairs={{1,0},{2,1},{3,2},{4,3},{5,4},{6,5},{7,6},{9,8},{10,9},{11,10},{12... | collective-permute-start | bytes 294920 | tf_op jit(solution)/shard_map/ppermute | solution.py:20
  92.1 2.1 collective-permute-start.3
  94.6 2.0 collective-permute-done.3
  96.6 0.8 pad_maximum_fusion
  99.2 1.7 fusion.5
  100.9 1.9 collective-permute-start.5
  102.8 4.3 %collective-permute-start.4 = (bf16[64,1,4,128]{3,0,2,1:T(8,128)(2,1)S(1)}, bf16[64,1,4,128]{3,0,2,1:T(8,128)(2,1)S(1)}, u32[]{:S(2)}, u32[]{:S(2)}) collective-permute-start(bf16[64,1,4,128]{3,0,2,1:T(8,128)(2,1)S(1)} %get-tuple-element.95), channel_id=1, source_target_pairs={{0,8},{8,16},{16,24},{1,9},{9,17},{17,25},{2,10},{10,18},{18,26},{... | collective-permute-start | bytes 196616 | tf_op jit(solution)/shard_map/ppermute | solution.py:19
  107.1 1.5 collective-permute-done.4
  108.7 2.0 collective-permute-start.6
  110.7 5.2 %collective-permute-start.7 = (bf16[64,6,1,128]{3,0,2,1:T(8,128)(2,1)S(1)}, bf16[64,6,1,128]{3,0,2,1:T(8,128)(2,1)S(1)}, u32[]{:S(2)}, u32[]{:S(2)}) collective-permute-start(bf16[64,6,1,128]{3,0,2,1:T(8,128)(2,1)S(1)} %get-tuple-element.80), channel_id=1, source_target_pairs={{0,1},{1,2},{2,3},{3,4},{4,5},{5,6},{6,7},{8,9},{9,10},{10,11},{11... | collective-permute-start | bytes 294920 | tf_op jit(solution)/shard_map/ppermute | solution.py:19
  116.3 1.3 collective-permute-done.7
  118.0 2.5 %fusion.1 = f32[64,4,4,128]{3,0,2,1:T(8,128)} fusion(f32[64,4,4,128]{3,0,2,1:T(8,128)S(1)} %copy-done.2, bf16[4,4,4,128,128]{4,3,2,1,0:T(8,128)(2,1)S(1)} %copy-done, pred[4,4,4]{2,1,0:T(4,128)(4,1)S(1)} %copy-done.32, pred[4,4,4]{2,1,0:T(4,128)(4,1)S(1)} %copy-done.34, pred[4,4,4]{2,1,0:T(4,128)(4,1)S(1)} %copy-done.21, ...), kind=kOutput, calls=%fused_computation.10 | convolution fusion | flops 139067392 | bytes 5505600 | tf_op jit(solution)/shard_map/eyxkq,yxkpq->eyxp/dot_general | solution.py:75
  120.5 1.4 copy.86
  122.6 7.1 %all_gather.15 = bf16[64,512]{0,1:T(8,128)(2,1)S(1)} all-gather(bf16[64,128]{0,1:T(8,128)(2,1)S(1)} %fusion.123), channel_id=1, replica_groups=mesh['row'=4,'col'=8] {'row'}, dimensions={1}, use_global_device_ids=true | all-gather | bytes 81920 | tf_op jit(solution)/shard_map/all_gather | solution.py:95
  129.8 8.3 %convolution_convert_fusion.1 = bf16[64,1024]{1,0:T(8,128)(2,1)S(1)} fusion(bf16[64,512]{0,1:T(8,128)(2,1)S(1)} %all_gather.15, f32[1024]{0:T(1024)S(1)} %bitcast.75, f32[512]{0:T(512)S(1)} %bitcast.81, f32[1024]{0:T(1024)S(1)} %bitcast.77, f32[512]{0:T(512)S(1)} %bitcast.83, f32[1024]{0:T(1024)S(1)} %bitcast.73, f32[512]{0:T(512)S(1)} %bitcast.79), kind=kOutput, calls=%fused_computation.16 | convolution fusion | flops 73990144 | bytes 215040 | tf_op jit(solution)/shard_map/while/body/eval_jaxpr/dot_general | solution.py:57
  138.1 0.8 copy.93
  139.0 29.2 %reduce-scatter.9.cloned.1.call-done = bf16[128,64]{1,0:T(8,128)(2,1)} async-done(((bf16[1024,64]{1,0:T(8,128)(2,1)}), bf16[128,64]{1,0:T(8,128)(2,1)}) %reduce-scatter.9.cloned.1.call-update) | async-done | bytes 16400
  168.2 0.8 copy.94
  169.1 1.3 scatter_custom_fusion.1
  171.5 2.1 collective-permute-start.9
  173.6 4.0 %collective-permute-start.8 = (bf16[64,1,4,128]{3,2,1,0:T(4,128)(2,1)}, bf16[64,1,4,128]{3,2,1,0:T(4,128)(2,1)S(1)}, u32[]{:S(2)}, u32[]{:S(2)}) collective-permute-start(bf16[64,1,4,128]{3,2,1,0:T(4,128)(2,1)} %get-tuple-element.91), channel_id=1, source_target_pairs={{0,8},{8,16},{16,24},{1,9},{9,17},{17,25},{2,10},{10,18},{18,26},{... | collective-permute-start | bytes 196616 | tf_op jit(solution)/shard_map/ppermute | solution.py:19
  177.7 1.1 copy.74
  180.1 6.6 %collective-permute-start.10 = (bf16[64,6,1,128]{3,2,1,0:T(2,128)(2,1)S(1)}, bf16[64,6,1,128]{3,2,1,0:T(2,128)(2,1)S(1)}, u32[]{:S(2)}, u32[]{:S(2)}) collective-permute-start(bf16[64,6,1,128]{3,2,1,0:T(2,128)(2,1)S(1)} %get-tuple-element.75), channel_id=1, source_target_pairs={{1,0},{2,1},{3,2},{4,3},{5,4},{6,5},{7,6},{9,8},{10,9},{11,10},{12... | collective-permute-start | bytes 294920 | tf_op jit(solution)/shard_map/ppermute | solution.py:20
  186.8 2.1 collective-permute-start.11
  189.4 1.9 collective-permute-done.11
  193.5 1.7 fusion.4
  195.2 1.9 collective-permute-start.13
  197.2 4.8 %collective-permute-start.12 = (bf16[64,1,4,128]{3,0,2,1:T(8,128)(2,1)S(1)}, bf16[64,1,4,128]{3,0,2,1:T(8,128)(2,1)S(1)}, u32[]{:S(2)}, u32[]{:S(2)}) collective-permute-start(bf16[64,1,4,128]{3,0,2,1:T(8,128)(2,1)S(1)} %get-tuple-element.87), channel_id=1, source_target_pairs={{0,8},{8,16},{16,24},{1,9},{9,17},{17,25},{2,10},{10,18},{18,26},{... | collective-permute-start | bytes 196616 | tf_op jit(solution)/shard_map/ppermute | solution.py:19
  202.0 1.3 collective-permute-done.12
  203.3 1.9 collective-permute-start.14
  205.2 5.2 %collective-permute-start.15 = (bf16[64,6,1,128]{3,0,2,1:T(8,128)(2,1)S(1)}, bf16[64,6,1,128]{3,0,2,1:T(8,128)(2,1)S(1)}, u32[]{:S(2)}, u32[]{:S(2)}) collective-permute-start(bf16[64,6,1,128]{3,0,2,1:T(8,128)(2,1)S(1)} %get-tuple-element.72), channel_id=1, source_target_pairs={{0,1},{1,2},{2,3},{3,4},{4,5},{5,6},{6,7},{8,9},{9,10},{10,11},{11... | collective-permute-start | bytes 294920 | tf_op jit(solution)/shard_map/ppermute | solution.py:19
  210.8 1.3 collective-permute-done.15
  212.5 2.4 %fusion.3 = f32[64,4,4,128]{3,0,2,1:T(8,128)S(1)} fusion(f32[64,4,4,128]{3,0,2,1:T(8,128)S(1)} %copy-done.1, bf16[4,4,4,128,128]{4,3,2,1,0:T(8,128)(2,1)S(1)} %copy-done, pred[4,4,4]{2,1,0:T(4,128)(4,1)S(1)} %copy-done.33, pred[4,4,4]{2,1,0:T(4,128)(4,1)S(1)} %copy-done.35, pred[4,4,4]{2,1,0:T(4,128)(4,1)S(1)} %copy-done.21, ...), kind=kOutput, calls=%fused_computation.12 | convolution fusion | flops 139067392 | bytes 5505600 | tf_op jit(solution)/shard_map/eyxkq,yxkpq->eyxp/dot_general | solution.py:75
  215.0 1.3 copy.90
  216.3 1.1 copy.75
  217.4 1.9 gather_fusion.1
  (150 shorter events, 14.1 us)
Async XLA Ops:
  7.2 91.5 %copy-start = (bf16[4,4,4,128,128]{4,3,2,1,0:T(8,128)(2,1)S(1)}, bf16[4,4,4,128,128]{4,3,2,1,0:T(8,128)(2,1)}, u32[]{:S(2)}) copy-start(bf16[4,4,4,128,128]{4,3,2,1,0:T(8,128)(2,1)} %param.12) | copy-start | bytes 6291460
  7.2 65.4 %reduce-scatter.7.cloned.1.call-start = ((), (), s32[]{:S(2)}) async-start(), calls=%async_computation.2 | async-start | bytes 294912
  33.2 9.3 %copy-start.38 = (s32[128]{0:T(128)S(1)}, s32[128]{0:T(128)}, u32[]{:S(2)}) copy-start(s32[128]{0:T(128)} %param.11) | copy-start | bytes 1540
  33.2 9.3 %copy-start.6 = (s32[4,4,4]{2,1,0:T(4,128)S(1)}, s32[4,4,4]{2,1,0:T(4,128)}, u32[]{:S(2)}) copy-start(s32[4,4,4]{2,1,0:T(4,128)} %param.13) | copy-start | bytes 772
  41.6 41.7 %copy-start.5 = (bf16[64,128]{1,0:T(8,128)(2,1)S(1)}, bf16[64,128]{1,0:T(8,128)(2,1)}, u32[]{:S(2)}) copy-start(bf16[64,128]{1,0:T(8,128)(2,1)} %param.9) | copy-start | bytes 49156
  42.5 125.7 %reduce-scatter.9.cloned.1.call-start = ((), (), s32[]{:S(2)}) async-start(), calls=%async_computation.3 | async-start | bytes 294912
  42.5 32.2 %copy-start.36 = (s32[128]{0:T(128)}, s32[128]{0:T(128)S(1)}, u32[]{:S(2)}) copy-start(s32[128]{0:T(128)S(1)} %compare_select_fusion) | copy-start | bytes 1540
  75.8 9.3 %collective-permute-start.1 = (bf16[64,1,4,128]{3,2,1,0:T(4,128)(2,1)}, bf16[64,1,4,128]{3,2,1,0:T(4,128)(2,1)S(1)}, u32[]{:S(2)}, u32[]{:S(2)}) collective-permute-start(bf16[64,1,4,128]{3,2,1,0:T(4,128)(2,1)} %get-tuple-element.100), channel_id=1, source_target_pairs={{8,0},{16,8},{24,16},{9,1},{17,9},{25,17},{10,2},{18,10},{26,18},{... | collective-permute-start | bytes 196616 | tf_op jit(solution)/shard_map/ppermute | solution.py:20
  77.8 7.4 %collective-permute-start = (bf16[64,1,4,128]{3,2,1,0:T(4,128)(2,1)}, bf16[64,1,4,128]{3,2,1,0:T(4,128)(2,1)S(1)}, u32[]{:S(2)}, u32[]{:S(2)}) collective-permute-start(bf16[64,1,4,128]{3,2,1,0:T(4,128)(2,1)} %get-tuple-element.99), channel_id=1, source_target_pairs={{0,8},{8,16},{16,24},{1,9},{9,17},{17,25},{2,10},{10,18},{18,26},{... | collective-permute-start | bytes 196616 | tf_op jit(solution)/shard_map/ppermute | solution.py:19
  85.8 8.9 %collective-permute-start.2 = (bf16[64,6,1,128]{3,2,1,0:T(2,128)(2,1)S(1)}, bf16[64,6,1,128]{3,2,1,0:T(2,128)(2,1)S(1)}, u32[]{:S(2)}, u32[]{:S(2)}) collective-permute-start(bf16[64,6,1,128]{3,2,1,0:T(2,128)(2,1)S(1)} %get-tuple-element.83), channel_id=1, source_target_pairs={{1,0},{2,1},{3,2},{4,3},{5,4},{6,5},{7,6},{9,8},{10,9},{11,10},{12... | collective-permute-start | bytes 294920 | tf_op jit(solution)/shard_map/ppermute | solution.py:20
  92.1 4.5 %collective-permute-start.3 = (bf16[64,6,1,128]{3,2,1,0:T(2,128)(2,1)S(1)}, bf16[64,6,1,128]{3,2,1,0:T(2,128)(2,1)S(1)}, u32[]{:S(2)}, u32[]{:S(2)}) collective-permute-start(bf16[64,6,1,128]{3,2,1,0:T(2,128)(2,1)S(1)} %get-tuple-element.84), channel_id=1, source_target_pairs={{0,1},{1,2},{2,3},{3,4},{4,5},{5,6},{6,7},{8,9},{9,10},{10,11},{11... | collective-permute-start | bytes 294920 | tf_op jit(solution)/shard_map/ppermute | solution.py:19
  98.1 1.0 copy-start.2
  98.1 1.0 copy-start.20
  98.1 1.0 copy-start.21
  98.1 1.0 copy-start.22
  98.1 1.0 copy-start.24
  98.1 1.0 copy-start.26
  98.1 1.0 copy-start.28
  98.2 1.0 copy-start.30
  98.2 1.0 copy-start.32
  98.2 1.0 copy-start.34
  99.2 7.9 %copy-start.37 = (s32[128]{0:T(128)S(1)}, s32[128]{0:T(128)}, u32[]{:S(2)}) copy-start(s32[128]{0:T(128)} %copy-done.36) | copy-start | bytes 1540
  100.9 6.2 %collective-permute-start.5 = (bf16[64,1,4,128]{3,0,2,1:T(8,128)(2,1)S(1)}, bf16[64,1,4,128]{3,0,2,1:T(8,128)(2,1)S(1)}, u32[]{:S(2)}, u32[]{:S(2)}) collective-permute-start(bf16[64,1,4,128]{3,0,2,1:T(8,128)(2,1)S(1)} %get-tuple-element.96), channel_id=1, source_target_pairs={{8,0},{16,8},{24,16},{9,1},{17,9},{25,17},{10,2},{18,10},{26,18},{... | collective-permute-start | bytes 196616 | tf_op jit(solution)/shard_map/ppermute | solution.py:20
  102.8 5.9 %collective-permute-start.4 = (bf16[64,1,4,128]{3,0,2,1:T(8,128)(2,1)S(1)}, bf16[64,1,4,128]{3,0,2,1:T(8,128)(2,1)S(1)}, u32[]{:S(2)}, u32[]{:S(2)}) collective-permute-start(bf16[64,1,4,128]{3,0,2,1:T(8,128)(2,1)S(1)} %get-tuple-element.95), channel_id=1, source_target_pairs={{0,8},{8,16},{16,24},{1,9},{9,17},{17,25},{2,10},{10,18},{18,26},{... | collective-permute-start | bytes 196616 | tf_op jit(solution)/shard_map/ppermute | solution.py:19
  108.7 7.5 %collective-permute-start.6 = (bf16[64,6,1,128]{3,0,2,1:T(8,128)(2,1)S(1)}, bf16[64,6,1,128]{3,0,2,1:T(8,128)(2,1)S(1)}, u32[]{:S(2)}, u32[]{:S(2)}) collective-permute-start(bf16[64,6,1,128]{3,0,2,1:T(8,128)(2,1)S(1)} %get-tuple-element.79), channel_id=1, source_target_pairs={{1,0},{2,1},{3,2},{4,3},{5,4},{6,5},{7,6},{9,8},{10,9},{11,10},{12... | collective-permute-start | bytes 294920 | tf_op jit(solution)/shard_map/ppermute | solution.py:20
  110.7 6.8 %collective-permute-start.7 = (bf16[64,6,1,128]{3,0,2,1:T(8,128)(2,1)S(1)}, bf16[64,6,1,128]{3,0,2,1:T(8,128)(2,1)S(1)}, u32[]{:S(2)}, u32[]{:S(2)}) collective-permute-start(bf16[64,6,1,128]{3,0,2,1:T(8,128)(2,1)S(1)} %get-tuple-element.80), channel_id=1, source_target_pairs={{0,1},{1,2},{2,3},{3,4},{4,5},{5,6},{6,7},{8,9},{9,10},{10,11},{11... | collective-permute-start | bytes 294920 | tf_op jit(solution)/shard_map/ppermute | solution.py:19
  118.0 4.5 %copy-start.3 = (bf16[64,128]{0,1:T(8,128)(2,1)S(1)}, bf16[64,128]{0,1:T(8,128)(2,1)}, u32[]{:S(2)}) copy-start(bf16[64,128]{0,1:T(8,128)(2,1)} %copy.46) | copy-start | bytes 49156
  118.0 4.5 %copy-start.13 = (pred[128]{0:T(512)(128)(4,1)S(1)}, pred[128]{0:T(512)(128)(4,1)}, u32[]{:S(2)}) copy-start(pred[128]{0:T(512)(128)(4,1)} %compare_and_fusion) | copy-start | bytes 388
  120.4 9.3 %copy-start.8 = (f32[1,1024]{1,0:T(1,128)S(1)}, f32[1,1024]{1,0:T(1,128)}, u32[]{:S(2)}) copy-start(f32[1,1024]{1,0:T(1,128)} %copy-done.7) | copy-start | bytes 12292
  120.4 9.3 %copy-start.10 = (f32[1,1024]{1,0:T(1,128)S(1)}, f32[1,1024]{1,0:T(1,128)}, u32[]{:S(2)}) copy-start(f32[1,1024]{1,0:T(1,128)} %copy-done.9) | copy-start | bytes 12292
  120.4 9.3 %copy-start.12 = (f32[1,1024]{1,0:T(1,128)S(1)}, f32[1,1024]{1,0:T(1,128)}, u32[]{:S(2)}) copy-start(f32[1,1024]{1,0:T(1,128)} %copy-done.11) | copy-start | bytes 12292
  120.4 9.3 %copy-start.15 = (f32[1,512]{1,0:T(1,128)S(1)}, f32[1,512]{1,0:T(1,128)}, u32[]{:S(2)}) copy-start(f32[1,512]{1,0:T(1,128)} %copy-done.14) | copy-start | bytes 6148
  120.4 9.3 %copy-start.17 = (f32[1,512]{1,0:T(1,128)S(1)}, f32[1,512]{1,0:T(1,128)}, u32[]{:S(2)}) copy-start(f32[1,512]{1,0:T(1,128)} %copy-done.16) | copy-start | bytes 6148
  120.4 9.3 %copy-start.19 = (f32[1,512]{1,0:T(1,128)S(1)}, f32[1,512]{1,0:T(1,128)}, u32[]{:S(2)}) copy-start(f32[1,512]{1,0:T(1,128)} %copy-done.18) | copy-start | bytes 6148
  171.5 7.4 %collective-permute-start.9 = (bf16[64,1,4,128]{3,2,1,0:T(4,128)(2,1)}, bf16[64,1,4,128]{3,2,1,0:T(4,128)(2,1)S(1)}, u32[]{:S(2)}, u32[]{:S(2)}) collective-permute-start(bf16[64,1,4,128]{3,2,1,0:T(4,128)(2,1)} %get-tuple-element.92), channel_id=1, source_target_pairs={{8,0},{16,8},{24,16},{9,1},{17,9},{25,17},{10,2},{18,10},{26,18},{... | collective-permute-start | bytes 196616 | tf_op jit(solution)/shard_map/ppermute | solution.py:20
  173.6 5.9 %collective-permute-start.8 = (bf16[64,1,4,128]{3,2,1,0:T(4,128)(2,1)}, bf16[64,1,4,128]{3,2,1,0:T(4,128)(2,1)S(1)}, u32[]{:S(2)}, u32[]{:S(2)}) collective-permute-start(bf16[64,1,4,128]{3,2,1,0:T(4,128)(2,1)} %get-tuple-element.91), channel_id=1, source_target_pairs={{0,8},{8,16},{16,24},{1,9},{9,17},{17,25},{2,10},{10,18},{18,26},{... | collective-permute-start | bytes 196616 | tf_op jit(solution)/shard_map/ppermute | solution.py:19
  180.1 9.2 %collective-permute-start.10 = (bf16[64,6,1,128]{3,2,1,0:T(2,128)(2,1)S(1)}, bf16[64,6,1,128]{3,2,1,0:T(2,128)(2,1)S(1)}, u32[]{:S(2)}, u32[]{:S(2)}) collective-permute-start(bf16[64,6,1,128]{3,2,1,0:T(2,128)(2,1)S(1)} %get-tuple-element.75), channel_id=1, source_target_pairs={{1,0},{2,1},{3,2},{4,3},{5,4},{6,5},{7,6},{9,8},{10,9},{11,10},{12... | collective-permute-start | bytes 294920 | tf_op jit(solution)/shard_map/ppermute | solution.py:20
  186.8 4.5 %collective-permute-start.11 = (bf16[64,6,1,128]{3,2,1,0:T(2,128)(2,1)S(1)}, bf16[64,6,1,128]{3,2,1,0:T(2,128)(2,1)S(1)}, u32[]{:S(2)}, u32[]{:S(2)}) collective-permute-start(bf16[64,6,1,128]{3,2,1,0:T(2,128)(2,1)S(1)} %get-tuple-element.76), channel_id=1, source_target_pairs={{0,1},{1,2},{2,3},{3,4},{4,5},{5,6},{6,7},{8,9},{9,10},{10,11},{11... | collective-permute-start | bytes 294920 | tf_op jit(solution)/shard_map/ppermute | solution.py:19
  192.4 1.0 copy-start.1
  192.5 1.0 copy-start.23
  192.5 1.0 copy-start.25
  192.5 1.0 copy-start.27
  192.5 1.0 copy-start.29
  195.2 6.7 %collective-permute-start.13 = (bf16[64,1,4,128]{3,0,2,1:T(8,128)(2,1)S(1)}, bf16[64,1,4,128]{3,0,2,1:T(8,128)(2,1)S(1)}, u32[]{:S(2)}, u32[]{:S(2)}) collective-permute-start(bf16[64,1,4,128]{3,0,2,1:T(8,128)(2,1)S(1)} %get-tuple-element.88), channel_id=1, source_target_pairs={{8,0},{16,8},{24,16},{9,1},{17,9},{25,17},{10,2},{18,10},{26,18},{... | collective-permute-start | bytes 196616 | tf_op jit(solution)/shard_map/ppermute | solution.py:20
  197.2 6.1 %collective-permute-start.12 = (bf16[64,1,4,128]{3,0,2,1:T(8,128)(2,1)S(1)}, bf16[64,1,4,128]{3,0,2,1:T(8,128)(2,1)S(1)}, u32[]{:S(2)}, u32[]{:S(2)}) collective-permute-start(bf16[64,1,4,128]{3,0,2,1:T(8,128)(2,1)S(1)} %get-tuple-element.87), channel_id=1, source_target_pairs={{0,8},{8,16},{16,24},{1,9},{9,17},{17,25},{2,10},{10,18},{18,26},{... | collective-permute-start | bytes 196616 | tf_op jit(solution)/shard_map/ppermute | solution.py:19
  203.3 7.5 %collective-permute-start.14 = (bf16[64,6,1,128]{3,0,2,1:T(8,128)(2,1)S(1)}, bf16[64,6,1,128]{3,0,2,1:T(8,128)(2,1)S(1)}, u32[]{:S(2)}, u32[]{:S(2)}) collective-permute-start(bf16[64,6,1,128]{3,0,2,1:T(8,128)(2,1)S(1)} %get-tuple-element.71), channel_id=1, source_target_pairs={{1,0},{2,1},{3,2},{4,3},{5,4},{6,5},{7,6},{9,8},{10,9},{11,10},{12... | collective-permute-start | bytes 294920 | tf_op jit(solution)/shard_map/ppermute | solution.py:20
  205.2 6.9 %collective-permute-start.15 = (bf16[64,6,1,128]{3,0,2,1:T(8,128)(2,1)S(1)}, bf16[64,6,1,128]{3,0,2,1:T(8,128)(2,1)S(1)}, u32[]{:S(2)}, u32[]{:S(2)}) collective-permute-start(bf16[64,6,1,128]{3,0,2,1:T(8,128)(2,1)S(1)} %get-tuple-element.72), channel_id=1, source_target_pairs={{0,1},{1,2},{2,3},{3,4},{4,5},{5,6},{6,7},{8,9},{9,10},{10,11},{11... | collective-permute-start | bytes 294920 | tf_op jit(solution)/shard_map/ppermute | solution.py:19
  214.9 4.4 %copy-start.4 = (bf16[64,128]{0,1:T(8,128)(2,1)S(1)}, bf16[64,128]{0,1:T(8,128)(2,1)}, u32[]{:S(2)}) copy-start(bf16[64,128]{0,1:T(8,128)(2,1)} %copy.46) | copy-start | bytes 49156
  (9 other events, 6.6 us)
Sparse Core Ops, SparseCore 0:
  42.6 29.9 reduce-scatter.6
  139.1 29.0 reduce-scatter.8
where the time goes:
time: 230 us; the launch traced here: 227 us
  waiting for transfers between devices  69.3 us (30%)
  starting transfers between devices  56.8 us (25%)
  blocking collectives  32.5 us (14%)
  matrix products  24.9 us (11%)
  local copies, waits for them, and re-layouts  23.3 us (10%)
  between operations  15.1 us (7%)
  other arithmetic  5.1 us (2%)
    unnamed x4, waiting for transfers between devices  58.7 us
    ppermute x8, starting transfers between devices, with_halo(): before = lax.ppermute(last, axis, up)  31.9 us
    ppermute x8, starting transfers between devices, with_halo(): after = lax.ppermute(initial, axis, down)  24.8 us
    dot_general x2, matrix products, add_block(): update = jnp.dot(piece, kernel, preferred_element_type=jnp.float32)  16.6 us
    all_gather x1, blocking collectives, per_device(): along_col = lax.all_gather(points, 'col', axis=1, tiled=True)  13.7 us
    all_gather x2, blocking collectives, per_device(): lax.all_gather(present, 'row', axis=1, tiled=True)  12.7 us
    ppermute x8, waiting for transfers between devices, with_halo(): before = lax.ppermute(last, axis, up)  9.94 us
    dot_general x4, matrix products, apply_tiles(): jnp.einsum('eyxkq,yxkpq->eyxp', picked, volume_tiles, preferred_element_t...  8.23 us
  transfers between devices with their start and end apart: 18, of which 11 were waited for; matrix products, arithmetic and copies ran while one was open for 3% of the time, Pallas kernels for 0%

commit v1 on v0

v1 whole, which is shorter than its diff:
```python
import functools
import math

import jax
import jax.numpy as jnp
import numpy as np
from jax import lax
from jax.experimental import pallas as pl
from jax.experimental.pallas import tpu as pltpu
from jax.sharding import PartitionSpec as P

OUTER_STEPS = 2
MESH = pl.DeviceIdType.MESH
NEIGHBOURS = ((-1, 0), (1, 0), (-1, -1), (-1, 1), (1, -1), (1, 1), (0, -1), (0, 1))
CHUNK = 16


def cosine_terms(degree):
    grid = 0.125 * (1.0 - np.cos(np.pi * (np.arange(400) + 0.5) / 400))
    fit = np.polynomial.Chebyshev.fit(grid, np.cos(2 * np.pi * np.sqrt(grid)), degree, domain=[0, 0.25])
    return [float(term) for term in fit.convert(kind=np.polynomial.Polynomial).coef]


def slot_of(dy, dx):
    return (dy + 1) * 3 + dx + 1


def edge_range(step, size):
    if step == 0:
        return list(range(size))
    return [size - 1] if step < 0 else [0]


def body(
    n_row, n_col, total, tiles_y, tiles_x, tile_count,
    columns, traces, incident, points, coupling, volume,
    traces_out, field_out,
    meta_own, meta_plane, meta_z, meta_halo, cols, kernel, hot_own, hot_halo, tiles,
    pres, gath, part, parts_in, curr, curr_halo, source, padded, own_one, pad_two, own_two, flat,
    load_sem, meta_plane_s, meta_plane_r, meta_z_s, meta_z_r, meta_halo_s, meta_halo_r,
    gath_s, gath_r, part_s, part_r, curr_s, curr_r, field_s, field_r,
):
    excite, shard = traces.shape
    group, depth = 2 * n_row, n_col // 2
    row, col = lax.axis_index("row"), lax.axis_index("col")
    z, core = col // 2, col % 2
    place = row * 2 + core
    wide = tiles_x + 2

    def plane_peer(step):
        other = (place + step) % group
        return (other // 2, z * 2 + other % 2)

    def z_peer(step):
        return (row, ((z + step) % depth) * 2 + core)

    def has(dy, dx):
        fine = None
        for step, index, size in ((dy, row, n_row), (dx, col, n_col)):
            if step != 0:
                good = index > 0 if step < 0 else index < size - 1
                fine = good if fine is None else jnp.logical_and(fine, good)
        return fine

    def send(src, dst, send_sem, recv_sem, device):
        return pltpu.make_async_remote_copy(
            src_ref=src, dst_ref=dst, send_sem=send_sem, recv_sem=recv_sem,
            device_id=device, device_id_type=MESH,
        )

    load = pltpu.make_async_copy(volume, tiles, load_sem)
    load.start()

    meta_halo[...] = jnp.zeros_like(meta_halo)
    curr_halo[...] = jnp.zeros_like(curr_halo)
    for outer in range(OUTER_STEPS):
        for y in range(tiles_y + 2):
            for x in range(tiles_x + 2):
                if y in (0, tiles_y + 1) or x in (0, tiles_x + 1):
                    pad_two[outer, y, x] = jnp.zeros((excite, shard), jnp.bfloat16)
    meta_own[...] = jnp.concatenate(
        [points[...], coupling[...].astype(jnp.float32), jnp.zeros((4, shard), jnp.float32)], axis=0
    )
    pres[0] = traces[...]
    meta_plane[0] = meta_own[...]
    meta_z[0] = meta_own[...]
    gath[0, 0] = traces[...]

    barrier = pltpu.get_barrier_semaphore()

    def greet(device):
        pl.semaphore_signal(barrier, inc=1, device_id=device, device_id_type=MESH)

    for step in range(1, group):
        greet(plane_peer(step))
    for step in range(1, depth):
        greet(z_peer(step))
    expected = jnp.int32(group - 1 + depth - 1)
    for dy, dx in NEIGHBOURS:
        there = has(dy, dx)
        pl.when(there)(functools.partial(greet, (row + dy, col + dx)))
        expected = expected + jnp.where(there, 1, 0)
    pl.semaphore_wait(barrier, expected)

    def meta_plane_copy(step):
        return send(meta_own, meta_plane.at[step], meta_plane_s.at[step], meta_plane_r.at[step], plane_peer(step))

    def meta_z_copy(step):
        return send(meta_own, meta_z.at[step], meta_z_s.at[step], meta_z_r.at[step], z_peer(step))

    def meta_halo_copy(dy, dx):
        mine, theirs = slot_of(dy, dx), slot_of(-dy, -dx)
        return send(meta_own, meta_halo.at[theirs], meta_halo_s.at[mine], meta_halo_r.at[theirs], (row + dy, col + dx))

    def meta_halo_arrival(dy, dx):
        mine = slot_of(dy, dx)
        return send(meta_own, meta_halo.at[mine], meta_halo_s.at[mine], meta_halo_r.at[mine], (row + dy, col + dx))

    def gath_copy(outer, step):
        return send(pres.at[outer], gath.at[outer, step], gath_s.at[outer, step], gath_r.at[outer, step], plane_peer(step))

    def part_copy(outer, step):
        return send(part.at[outer, step], parts_in.at[outer, step], part_s.at[outer, step], part_r.at[outer, step], z_peer(-step))

    def curr_copy(outer, dy, dx, slot):
        return send(
            curr.at[outer], curr_halo.at[outer, slot], curr_s.at[outer, slot_of(dy, dx)],
            curr_r.at[outer, slot], (row + dy, col + dx),
        )

    def field_copy(outer, dy, dx, arrival):
        side = (dy, dx) if arrival else (-dy, -dx)
        ranges, sources = [], []
        for step, out_step, size in ((side[0], dy, tiles_y), (side[1], dx, tiles_x)):
            ranges.append(pl.ds(1, size) if step == 0 else pl.ds(0 if step < 0 else size + 1, 1))
            sources.append(pl.ds(0, size) if out_step == 0 else pl.ds(0 if out_step < 0 else size - 1, 1))
        slot = slot_of(*side)
        return send(
            own_two.at[outer, sources[0], sources[1]], pad_two.at[outer, ranges[0], ranges[1]],
            field_s.at[outer, slot_of(dy, dx)], field_r.at[outer, slot], (row + dy, col + dx),
        )

    for step in range(1, group):
        meta_plane_copy(step).start()
    for step in range(1, depth):
        meta_z_copy(step).start()
    for step in range(1, group):
        gath_copy(0, step).start()
    for dy, dx in NEIGHBOURS:
        pl.when(has(dy, dx))(lambda dy=dy, dx=dx: meta_halo_copy(dy, dx).start())

    lanes = lax.broadcasted_iota(jnp.int32, (shard, shard), 1).astype(jnp.float32)

    def one_hot(column, tile):
        return jnp.where(column == lanes + float(tile * shard), 1.0, 0.0).astype(jnp.bfloat16)

    own_column = jnp.broadcast_to(meta_own[...].T[:, 3:4], (shard, shard))
    for tile in range(tiles_y * tiles_x):
        hot_own[:, tile * shard:(tile + 1) * shard] = one_hot(own_column, tile)

    for step in range(1, group):
        meta_plane_copy(step).wait_recv()
    for step in range(1, depth):
        meta_z_copy(step).wait_recv()

    wave = 2.0 * float(total) ** (1.0 / 3.0)
    smooth = (0.5 * float(total) ** (-1.0 / 3.0)) ** 2
    factor = 1.0 / math.sqrt(2.0 * total)
    terms = [factor * term for term in cosine_terms(5)]
    for step in range(group):
        cols[step * shard:(step + 1) * shard, :] = meta_plane[step].T
    targets = [jnp.concatenate([meta_z[step, d:d + 1, :] for step in range(depth)], axis=1) for d in range(3)]

    def build(number, carry):
        rows = pl.ds(pl.multiple_of(number * CHUNK, CHUNK), CHUNK)
        mine = cols[rows, :]
        square = smooth
        for d in range(3):
            delta = mine[:, d:d + 1] - targets[d]
            square = square + delta * delta
        inverse = lax.rsqrt(square)
        turns = (wave / (2.0 * math.pi)) * (square * inverse)
        turns = turns - jnp.floor(turns + 0.5)
        turns = turns * turns
        value = terms[-1]
        for term in terms[-2::-1]:
            value = value * turns + term
        kernel[rows, :] = (value * inverse).astype(jnp.bfloat16)
        return carry

    lax.fori_loop(0, group * shard // CHUNK, build, 0, unroll=2)

    halo_places, number = {}, 0
    for dy, dx in NEIGHBOURS:
        pl.when(has(dy, dx))(lambda dy=dy, dx=dx: meta_halo_arrival(dy, dx).wait_recv())
        column = jnp.broadcast_to(meta_halo[slot_of(dy, dx)].T[:, 3:4], (shard, shard))
        places = []
        for y in edge_range(dy, tiles_y):
            for x in edge_range(dx, tiles_x):
                hot_halo[:, number * shard:(number + 1) * shard] = one_hot(column, y * tiles_x + x)
                to_y = y + 1 if dy == 0 else (0 if dy < 0 else tiles_y + 1)
                to_x = x + 1 if dx == 0 else (0 if dx < 0 else tiles_x + 1)
                places.append((number, to_y, to_x))
                number += 1
        halo_places[(dy, dx)] = places

    load.wait()

    def pick(ref_index, ref, y, x, stride, shift):
        picked = []
        for k in range(tile_count):
            offset = columns[(y * tiles_x + x) * tile_count + k]
            at = (y + offset // 3 - shift) * stride + x + offset % 3 - shift
            picked.append(ref[at] if ref_index is None else ref[ref_index, at])
        return jnp.concatenate(picked, axis=1)

    def apply(picked, y, x):
        acc = source[y * tiles_x + x]
        for k in range(tile_count):
            acc = acc + lax.dot_general(
                picked[:, k * shard:(k + 1) * shard], tiles[y, x, k], (((1,), (1,)), ((), ())),
                preferred_element_type=jnp.float32,
            )
        return acc

    inner = [(y, x) for y in range(1, tiles_y - 1) for x in range(1, tiles_x - 1)]
    outside = [(y, x) for y in range(tiles_y) for x in range(tiles_x) if (y, x) not in inner]

    def outer_step(outer):
        for step in range(1, group):
            gath_copy(outer, step).wait_recv()
        gathered = jnp.concatenate([gath[outer, step] for step in range(group)], axis=1)
        sums = jnp.dot(gathered, kernel[...], preferred_element_type=jnp.float32)
        for step in range(1, depth):
            part[outer, step] = sums[:, step * shard:(step + 1) * shard].astype(jnp.bfloat16)
        for step in range(1, depth):
            part_copy(outer, step).start()
        current = sums[:, :shard]
        for step in range(1, depth):
            part_copy(outer, step).wait_recv()
            current = current + parts_in[outer, step].astype(jnp.float32)
        rounded = current.astype(jnp.bfloat16)
        curr[outer] = rounded
        for dy, dx in NEIGHBOURS:
            pl.when(has(dy, dx))(lambda dy=dy, dx=dx: curr_copy(outer, dy, dx, slot_of(-dy, -dx)).start())

        spread = jnp.dot(rounded, hot_own[...], preferred_element_type=jnp.float32)
        for y in range(tiles_y):
            for x in range(tiles_x):
                tile = y * tiles_x + x
                value = spread[:, tile * shard:(tile + 1) * shard]
                source[tile] = value
                value = value.astype(jnp.bfloat16)
                padded[(y + 1) * wide + x + 1] = value
                own_one[tile] = value
        for y, x in inner:
            own_two[outer, y, x] = apply(pick(None, own_one, y, x, tiles_x, 1), y, x).astype(jnp.bfloat16)
        for dy, dx in NEIGHBOURS:
            pl.when(has(dy, dx))(lambda dy=dy, dx=dx: curr_copy(outer, dy, dx, slot_of(dy, dx)).wait_recv())
            places = halo_places[(dy, dx)]
            first = places[0][0]
            halo = jnp.dot(
                curr_halo[outer, slot_of(dy, dx)], hot_halo[:, first * shard:(first + len(places)) * shard],
                preferred_element_type=jnp.float32,
            ).astype(jnp.bfloat16)
            for number, y, x in places:
                padded[y * wide + x] = halo[:, (number - first) * shard:(number - first + 1) * shard]
        for y, x in outside:
            own_two[outer, y, x] = apply(pick(None, padded, y, x, wide, 0), y, x).astype(jnp.bfloat16)
        for dy, dx in NEIGHBOURS:
            pl.when(has(dy, dx))(lambda dy=dy, dx=dx: field_copy(outer, dy, dx, False).start())
        for y in range(tiles_y):
            for x in range(tiles_x):
                value = own_two[outer, y, x]
                own_one[y * tiles_x + x] = value
                padded[(y + 1) * wide + x + 1] = value

        def finish(ref, y, x, stride, shift):
            tile = y * tiles_x + x
            value = apply(pick(None, ref, y, x, stride, shift), y, x)
            field_out[tile] = value
            flat[:, tile * shard:(tile + 1) * shard] = value.astype(jnp.bfloat16)

        for y, x in inner:
            finish(own_one, y, x, tiles_x, 1)
        for dy, dx in NEIGHBOURS:
            pl.when(has(dy, dx))(lambda dy=dy, dx=dx: field_copy(outer, dy, dx, True).wait_recv())
        for y in range(tiles_y + 2):
            for x in range(tiles_x + 2):
                if y in (0, tiles_y + 1) or x in (0, tiles_x + 1):
                    padded[y * wide + x] = pad_two[outer, y, x]
        for y, x in outside:
            finish(padded, y, x, wide, 0)
        readout = lax.dot_general(
            flat[...], hot_own[...], (((1,), (1,)), ((), ())), preferred_element_type=jnp.float32
        )
        present = (incident[...].astype(jnp.float32) + readout).astype(jnp.bfloat16)
        traces_out[...] = present

        if outer + 1 < OUTER_STEPS:
            pres[outer + 1] = present
            gath[outer + 1, 0] = present
            for step in range(1, group):
                gath_copy(outer + 1, step).start()

        for step in range(1, group):
            gath_copy(outer, step).wait_send()
        for step in range(1, depth):
            part_copy(outer, step).wait_send()
        for dy, dx in NEIGHBOURS:
            pl.when(has(dy, dx))(lambda dy=dy, dx=dx: curr_copy(outer, dy, dx, slot_of(-dy, -dx)).wait_send())
            pl.when(has(dy, dx))(lambda dy=dy, dx=dx: field_copy(outer, dy, dx, False).wait_send())

    for outer in range(OUTER_STEPS):
        outer_step(outer)
    for step in range(1, group):
        meta_plane_copy(step).wait_send()
    for step in range(1, depth):
        meta_z_copy(step).wait_send()
    for dy, dx in NEIGHBOURS:
        pl.when(has(dy, dx))(lambda dy=dy, dx=dx: meta_halo_copy(dy, dx).wait_send())


def per_device(n_row, n_col, traces, incident, points, coupling, volume_tiles, tile_columns):
    excite, shard = traces.shape
    total = shard * n_row * n_col
    tiles_y, tiles_x, tile_count, side, _ = volume_tiles.shape
    group, depth = 2 * n_row, n_col // 2
    count = tiles_y * tiles_x
    halo = 2 * (tiles_y + tiles_x) + 4
    dma = pltpu.SemaphoreType.DMA
    bf16, f32 = jnp.bfloat16, jnp.float32
    vmem = pl.BlockSpec(memory_space=pltpu.VMEM)
    steps = OUTER_STEPS
    present, field = pl.pallas_call(
        functools.partial(body, n_row, n_col, total, tiles_y, tiles_x, tile_count),
        out_shape=(
            jax.ShapeDtypeStruct((excite, shard), bf16),
            jax.ShapeDtypeStruct((count, excite, side), f32),
        ),
        in_specs=[pl.BlockSpec(memory_space=pltpu.SMEM), vmem, vmem, vmem, vmem, pl.BlockSpec(memory_space=pl.ANY)],
        out_specs=(vmem, vmem),
        scratch_shapes=[
            pltpu.VMEM((8, shard), f32),
            pltpu.VMEM((group, 8, shard), f32),
            pltpu.VMEM((depth, 8, shard), f32),
            pltpu.VMEM((9, 8, shard), f32),
            pltpu.VMEM((group * shard, 8), f32),
            pltpu.VMEM((group * shard, depth * shard), bf16),
            pltpu.VMEM((shard, count * side), bf16),
            pltpu.VMEM((shard, halo * side), bf16),
            pltpu.VMEM(volume_tiles.shape, bf16),
            pltpu.VMEM((steps, excite, shard), bf16),
            pltpu.VMEM((steps, group, excite, shard), bf16),
            pltpu.VMEM((steps, depth, excite, shard), bf16),
            pltpu.VMEM((steps, depth, excite, shard), bf16),
            pltpu.VMEM((steps, excite, shard), bf16),
            pltpu.VMEM((steps, 9, excite, shard), bf16),
            pltpu.VMEM((count, excite, side), f32),
            pltpu.VMEM(((tiles_y + 2) * (tiles_x + 2), excite, side), bf16),
            pltpu.VMEM((count, excite, side), bf16),
            pltpu.VMEM((steps, tiles_y + 2, tiles_x + 2, excite, side), bf16),
            pltpu.VMEM((steps, tiles_y, tiles_x, excite, side), bf16),
            pltpu.VMEM((excite, count * side), bf16),
            dma, dma((group,)), dma((group,)), dma((depth,)), dma((depth,)), dma((9,)), dma((9,)),
            dma((steps, group)), dma((steps, group)), dma((steps, depth)), dma((steps, depth)),
            dma((steps, 9)), dma((steps, 9)), dma((steps, 9)), dma((steps, 9)),
        ],
        compiler_params=pltpu.CompilerParams(
            collective_id=0, has_side_effects=True, vmem_limit_bytes=40 * 2**20
        ),
        cost_estimate=pl.CostEstimate(flops=10**9, bytes_accessed=4 * 2**20, transcendentals=0),
    )(tile_columns.reshape(-1), traces, incident, points, coupling.reshape(1, shard), volume_tiles)
    field = field.reshape(tiles_y, tiles_x, excite, side).transpose(2, 0, 1, 3)
    return (present, field)


def solution(mesh):
    in_specs = (
        P(None, ("row", "col")),
        P(None, ("row", "col")),
        P(None, ("row", "col")),
        P(("row", "col")),
        P("row", "col", None, None, None),
        P("row", "col", None),
    )
    out_specs = (P(None, ("row", "col")), P(None, "row", "col", None))
    return jax.shard_map(
        functools.partial(per_device, mesh.shape["row"], mesh.shape["col"]),
        mesh=mesh, in_specs=in_specs, out_specs=out_specs, check_vma=False,
    )
```

time: 230 us -> 60.8 us (0.26); the launches traced: 227 us -> 60.4 us
  waiting for transfers between devices: 69.3 us -> 0 us
  starting transfers between devices: 56.8 us -> 0 us
  Pallas kernels: 0 us -> 52.8 us
  blocking collectives: 32.5 us -> 0 us
  matrix products: 24.9 us -> 0 us
  local copies, waits for them, and re-layouts: 23.3 us -> 6.88 us
  between operations: 15.1 us -> 0.65 us
  other arithmetic: 5.1 us -> 0 us
    unnamed x4 -> x0, waiting for transfers between devices: 58.7 us -> none
    ppermute x16 -> x0, starting transfers between devices: 56.8 us -> none  [the longest x8 31.9 us: with_halo(): before = lax.ppermute(last, axis, up)]
    pallas_call x0 -> x1, Pallas kernels: none -> 52.8 us  [per_device(): pl.pallas_call(functools.partial(body, n_row, n_col, total, tiles_y, tile...]
    all_gather x4 -> x0, blocking collectives: 32.5 us -> none  [the longest x1 13.7 us: per_device(): along_col = lax.all_gather(points, 'col', axis=1, tiled=True)]
    dot_general x6 -> x0, matrix products: 24.9 us -> none  [the longest x2 16.6 us: add_block(): update = jnp.dot(piece, kernel, preferred_element_type=jnp.float32)]
    ppermute x16 -> x0, waiting for transfers between devices: 10.6 us -> none  [the longest x8 9.94 us: with_halo(): before = lax.ppermute(last, axis, up)]
    slice x31 -> x0, local copies, waits for them, and re-layouts: 5.11 us -> none  [the longest x23 3.14 us: apply_tiles(): view = padded[:, first:first + tiles_y, second:second + tiles_x, :]]
    reshape x6 -> x2, local copies, waits for them, and re-layouts: 5.72 us -> 1.92 us  [the longest x1 1.13 us: per_device(): field = field.reshape(tiles_y, tiles_x, excite, side).transpose(2, 0, 1, 3)]
  transfers between devices with their start and end apart: 18 -> 0, of which waited for: 11 -> 0; matrix products, arithmetic and copies ran while one was open for 3% -> 0% of each run, Pallas kernels for 0% -> 0%
where the time goes in v1:
time: 60.8 us; the launch traced here: 60.4 us
  Pallas kernels  52.8 us (87%)
  local copies, waits for them, and re-layouts  6.88 us (11%)
  between operations  0.65 us (1%)
    pallas_call x1, Pallas kernels, per_device(): pl.pallas_call(functools.partial(body, n_row, n_col, total, tiles_y, tile...  52.8 us
    unnamed x11, local copies, waits for them, and re-layouts  4.96 us

profile of v1, /device:TPU:3, one launch (start us, length us, event | category | flops | bytes accessed | tf_op | source)
XLA Modules:
  0.0 60.4 jit_solution(2263379854354350700)
XLA Ops:
  0.6 0.8 %reshape.13.columns = s32[64]{0:T(128)S(1)} reshape(s32[4,4,4]{2,1,0:T(4,128)} %param.11) | data formatting | bytes 512 | tf_op jit(solution)/shard_map/reshape | solution.py:373
  1.4 0.0 copy-start
  1.4 1.6 %copy-done = bf16[4,4,4,128,128]{4,3,2,1,0:T(8,128)(2,1)S(1)} copy-done((bf16[4,4,4,128,128]{4,3,2,1,0:T(8,128)(2,1)S(1)}, bf16[4,4,4,128,128]{4,3,2,1,0:T(8,128)(2,1)}, u32[]{:S(2)}) %copy-start) | copy-done | bytes 2097176
  3.0 0.0 copy-start.1
  3.0 0.7 %copy-done.1 = bf16[64,128]{1,0:T(8,128)(2,1)S(1)} copy-done((bf16[64,128]{1,0:T(8,128)(2,1)S(1)}, bf16[64,128]{1,0:T(8,128)(2,1)}, u32[]{:S(2)}) %copy-start.1) | copy-done | bytes 16408
  3.7 0.0 copy-start.2
  3.7 0.7 %copy-done.2 = bf16[64,128]{1,0:T(8,128)(2,1)S(1)} copy-done((bf16[64,128]{1,0:T(8,128)(2,1)S(1)}, bf16[64,128]{1,0:T(8,128)(2,1)}, u32[]{:S(2)}) %copy-start.2) | copy-done | bytes 16408
  4.4 0.0 copy-start.3
  4.5 0.7 %copy-done.3 = f32[3,128]{1,0:T(4,128)S(1)} copy-done((f32[3,128]{1,0:T(4,128)S(1)}, f32[3,128]{1,0:T(4,128)}, u32[]{:S(2)}) %copy-start.3) | copy-done | bytes 1560
  5.1 0.0 copy-start.4
  5.1 0.7 %copy-done.4 = s32[128]{0:T(128)S(1)} copy-done((s32[128]{0:T(128)S(1)}, s32[128]{0:T(128)}, u32[]{:S(2)}) %copy-start.4) | copy-done | bytes 536
  5.8 52.8 %shard_map.77 = (bf16[64,128]{1,0:T(8,128)(2,1)S(1)}, f32[16,64,128]{2,1,0:T(8,128)S(1)}) custom-call(s32[64]{0:T(128)S(1)} %reshape.13.columns, bf16[64,128]{1,0:T(8,128)(2,1)S(1)} %copy-done.1, bf16[64,128]{1,0:T(8,128)(2,1)S(1)} %copy-done.2, f32[3,128]{1,0:T(4,128)S(1)} %copy-done.3, s32[1,128]{1,0:T(1,128)S(1)} %bitcast.6, ...), custom_call_target="tpu_custom_call" | custom-call | flops 1000000000 | bytes 4194304 | tf_op jit(solution)/shard_map/pallas_call | solution.py:335
  58.6 1.1 %copy.10 = f32[4,4,64,128]{3,1,0,2:T(4,128)} copy(f32[4,4,64,128]{3,2,1,0:T(8,128)S(1)} %bitcast.5) | data formatting | bytes 1048576 | tf_op jit(solution)/shard_map/reshape | solution.py:374
  59.8 0.6 %copy.12 = bf16[64,128]{1,0:T(8,128)(2,1)} copy(bf16[64,128]{1,0:T(8,128)(2,1)S(1)} %get-tuple-element.8) | data formatting | bytes 32768
Async XLA Ops:
  1.4 1.6 %copy-start = (bf16[4,4,4,128,128]{4,3,2,1,0:T(8,128)(2,1)S(1)}, bf16[4,4,4,128,128]{4,3,2,1,0:T(8,128)(2,1)}, u32[]{:S(2)}) copy-start(bf16[4,4,4,128,128]{4,3,2,1,0:T(8,128)(2,1)} %volume.1) | copy-start | bytes 6291460
  3.0 0.7 %copy-start.1 = (bf16[64,128]{1,0:T(8,128)(2,1)S(1)}, bf16[64,128]{1,0:T(8,128)(2,1)}, u32[]{:S(2)}) copy-start(bf16[64,128]{1,0:T(8,128)(2,1)} %traces.1) | copy-start | bytes 49156
  3.7 0.7 %copy-start.2 = (bf16[64,128]{1,0:T(8,128)(2,1)S(1)}, bf16[64,128]{1,0:T(8,128)(2,1)}, u32[]{:S(2)}) copy-start(bf16[64,128]{1,0:T(8,128)(2,1)} %incident.1) | copy-start | bytes 49156
  4.4 0.7 %copy-start.3 = (f32[3,128]{1,0:T(4,128)S(1)}, f32[3,128]{1,0:T(4,128)}, u32[]{:S(2)}) copy-start(f32[3,128]{1,0:T(4,128)} %points.1) | copy-start | bytes 4612
  5.1 0.7 %copy-start.4 = (s32[128]{0:T(128)S(1)}, s32[128]{0:T(128)}, u32[]{:S(2)}) copy-start(s32[128]{0:T(128)} %param.9) | copy-start | bytes 1540

commit v2 on v1

--- a/solution.py
+++ b/solution.py
@@ -33,11 +33,11 @@
 
 def body(
     n_row, n_col, total, tiles_y, tiles_x, tile_count,
-    columns, traces, incident, points, coupling, volume,
+    columns, traces, incident_in, points_in, coupling_in, volume,
     traces_out, field_out,
-    meta_own, meta_plane, meta_z, meta_halo, cols, kernel, hot_own, hot_halo, tiles,
+    incident, points, coupling, hot_read, meta_own, meta_plane, meta_z, meta_halo, cols, kernel, hot_own, hot_halo, tiles,
     pres, gath, part, parts_in, curr, curr_halo, source, padded, own_one, pad_two, own_two, flat,
-    load_sem, meta_plane_s, meta_plane_r, meta_z_s, meta_z_r, meta_halo_s, meta_halo_r,
+    load_sem, small_sem, meta_plane_s, meta_plane_r, meta_z_s, meta_z_r, meta_halo_s, meta_halo_r,
     gath_s, gath_r, part_s, part_r, curr_s, curr_r, field_s, field_r,
 ):
     excite, shard = traces.shape
@@ -69,6 +69,14 @@
         )
 
     load = pltpu.make_async_copy(volume, tiles, load_sem)
+    small = [
+        pltpu.make_async_copy(src, dst, small_sem.at[number])
+        for number, (src, dst) in enumerate((
+            (traces, pres.at[0]), (points_in, points), (coupling_in, coupling), (incident_in, incident),
+        ))
+    ]
+    for copy in small:
+        copy.start()
     load.start()
 
     meta_halo[...] = jnp.zeros_like(meta_halo)
@@ -78,13 +86,14 @@
             for x in range(tiles_x + 2):
                 if y in (0, tiles_y + 1) or x in (0, tiles_x + 1):
                     pad_two[outer, y, x] = jnp.zeros((excite, shard), jnp.bfloat16)
+    for copy in small:
+        copy.wait()
     meta_own[...] = jnp.concatenate(
         [points[...], coupling[...].astype(jnp.float32), jnp.zeros((4, shard), jnp.float32)], axis=0
     )
-    pres[0] = traces[...]
     meta_plane[0] = meta_own[...]
     meta_z[0] = meta_own[...]
-    gath[0, 0] = traces[...]
+    gath[0, 0] = pres[0]
 
     barrier = pltpu.get_barrier_semaphore()
 
@@ -154,6 +163,12 @@
     def one_hot(column, tile):
         return jnp.where(column == lanes + float(tile * shard), 1.0, 0.0).astype(jnp.bfloat16)
 
+    rows_of = lax.broadcasted_iota(jnp.int32, (shard, shard), 0)
+    own_row = jnp.broadcast_to(coupling[...], (shard, shard))
+    for tile in range(tiles_y * tiles_x):
+        hot_read[tile * shard:(tile + 1) * shard, :] = jnp.where(
+            own_row == rows_of + tile * shard, 1.0, 0.0
+        ).astype(jnp.bfloat16)
     own_column = jnp.broadcast_to(meta_own[...].T[:, 3:4], (shard, shard))
     for tile in range(tiles_y * tiles_x):
         hot_own[:, tile * shard:(tile + 1) * shard] = one_hot(own_column, tile)
@@ -206,22 +221,13 @@
 
     load.wait()
 
-    def pick(ref_index, ref, y, x, stride, shift):
-        picked = []
-        for k in range(tile_count):
-            offset = columns[(y * tiles_x + x) * tile_count + k]
-            at = (y + offset // 3 - shift) * stride + x + offset % 3 - shift
-            picked.append(ref[at] if ref_index is None else ref[ref_index, at])
-        return jnp.concatenate(picked, axis=1)
-
-    def apply(picked, y, x):
-        acc = source[y * tiles_x + x]
-        for k in range(tile_count):
-            acc = acc + lax.dot_general(
-                picked[:, k * shard:(k + 1) * shard], tiles[y, x, k], (((1,), (1,)), ((), ())),
-                preferred_element_type=jnp.float32,
-            )
-        return acc
+    def apply(ref, y, x):
+        tile = y * tiles_x + x
+        picked = jnp.concatenate([ref[columns[tile * tile_count + k]] for k in range(tile_count)], axis=1)
+        matrix = jnp.concatenate([tiles[y, x, k] for k in range(tile_count)], axis=1)
+        return source[tile] + lax.dot_general(
+            picked, matrix, (((1,), (1,)), ((), ())), preferred_element_type=jnp.float32
+        )
 
     inner = [(y, x) for y in range(1, tiles_y - 1) for x in range(1, tiles_x - 1)]
     outside = [(y, x) for y in range(tiles_y) for x in range(tiles_x) if (y, x) not in inner]
@@ -252,9 +258,9 @@
                 source[tile] = value
                 value = value.astype(jnp.bfloat16)
                 padded[(y + 1) * wide + x + 1] = value
-                own_one[tile] = value
+                own_one[(y + 1) * wide + x + 1] = value
         for y, x in inner:
-            own_two[outer, y, x] = apply(pick(None, own_one, y, x, tiles_x, 1), y, x).astype(jnp.bfloat16)
+            own_two[outer, y, x] = apply(own_one, y, x).astype(jnp.bfloat16)
         for dy, dx in NEIGHBOURS:
             pl.when(has(dy, dx))(lambda dy=dy, dx=dx: curr_copy(outer, dy, dx, slot_of(dy, dx)).wait_recv())
             places = halo_places[(dy, dx)]
@@ -265,24 +271,27 @@
             ).astype(jnp.bfloat16)
             for number, y, x in places:
                 padded[y * wide + x] = halo[:, (number - first) * shard:(number - first + 1) * shard]
-        for y, x in outside:
-            own_two[outer, y, x] = apply(pick(None, padded, y, x, wide, 0), y, x).astype(jnp.bfloat16)
-        for dy, dx in NEIGHBOURS:
-            pl.when(has(dy, dx))(lambda dy=dy, dx=dx: field_copy(outer, dy, dx, False).start())
+        for sideways in (False, True):
+            for y, x in outside:
+                if (y in (0, tiles_y - 1)) != sideways:
+                    own_two[outer, y, x] = apply(padded, y, x).astype(jnp.bfloat16)
+            for dy, dx in NEIGHBOURS:
+                if (dy == 0) == sideways:
+                    pl.when(has(dy, dx))(lambda dy=dy, dx=dx: field_copy(outer, dy, dx, False).start())
         for y in range(tiles_y):
             for x in range(tiles_x):
                 value = own_two[outer, y, x]
-                own_one[y * tiles_x + x] = value
+                own_one[(y + 1) * wide + x + 1] = value
                 padded[(y + 1) * wide + x + 1] = value
 
-        def finish(ref, y, x, stride, shift):
+        def finish(ref, y, x):
             tile = y * tiles_x + x
-            value = apply(pick(None, ref, y, x, stride, shift), y, x)
+            value = apply(ref, y, x)
             field_out[tile] = value
             flat[:, tile * shard:(tile + 1) * shard] = value.astype(jnp.bfloat16)
 
         for y, x in inner:
-            finish(own_one, y, x, tiles_x, 1)
+            finish(own_one, y, x)
         for dy, dx in NEIGHBOURS:
             pl.when(has(dy, dx))(lambda dy=dy, dx=dx: field_copy(outer, dy, dx, True).wait_recv())
         for y in range(tiles_y + 2):
@@ -290,10 +299,8 @@
                 if y in (0, tiles_y + 1) or x in (0, tiles_x + 1):
                     padded[y * wide + x] = pad_two[outer, y, x]
         for y, x in outside:
-            finish(padded, y, x, wide, 0)
-        readout = lax.dot_general(
-            flat[...], hot_own[...], (((1,), (1,)), ((), ())), preferred_element_type=jnp.float32
-        )
+            finish(padded, y, x)
+        readout = jnp.dot(flat[...], hot_read[...], preferred_element_type=jnp.float32)
         present = (incident[...].astype(jnp.float32) + readout).astype(jnp.bfloat16)
         traces_out[...] = present
 
@@ -332,15 +339,22 @@
     bf16, f32 = jnp.bfloat16, jnp.float32
     vmem = pl.BlockSpec(memory_space=pltpu.VMEM)
     steps = OUTER_STEPS
+    ys = jnp.arange(tiles_y, dtype=jnp.int32)[:, None, None]
+    xs = jnp.arange(tiles_x, dtype=jnp.int32)[None, :, None]
+    places = (ys + tile_columns // 3) * (tiles_x + 2) + xs + tile_columns % 3
     present, field = pl.pallas_call(
         functools.partial(body, n_row, n_col, total, tiles_y, tiles_x, tile_count),
         out_shape=(
             jax.ShapeDtypeStruct((excite, shard), bf16),
             jax.ShapeDtypeStruct((count, excite, side), f32),
         ),
-        in_specs=[pl.BlockSpec(memory_space=pltpu.SMEM), vmem, vmem, vmem, vmem, pl.BlockSpec(memory_space=pl.ANY)],
+        in_specs=[pl.BlockSpec(memory_space=pltpu.SMEM)] + [pl.BlockSpec(memory_space=pltpu.HBM)] * 5,
         out_specs=(vmem, vmem),
         scratch_shapes=[
+            pltpu.VMEM((excite, shard), bf16),
+            pltpu.VMEM((3, shard), f32),
+            pltpu.VMEM((1, shard), jnp.int32),
+            pltpu.VMEM((count * side, shard), bf16),
             pltpu.VMEM((8, shard), f32),
             pltpu.VMEM((group, 8, shard), f32),
             pltpu.VMEM((depth, 8, shard), f32),
@@ -358,19 +372,19 @@
             pltpu.VMEM((steps, 9, excite, shard), bf16),
             pltpu.VMEM((count, excite, side), f32),
             pltpu.VMEM(((tiles_y + 2) * (tiles_x + 2), excite, side), bf16),
-            pltpu.VMEM((count, excite, side), bf16),
+            pltpu.VMEM(((tiles_y + 2) * (tiles_x + 2), excite, side), bf16),
             pltpu.VMEM((steps, tiles_y + 2, tiles_x + 2, excite, side), bf16),
             pltpu.VMEM((steps, tiles_y, tiles_x, excite, side), bf16),
             pltpu.VMEM((excite, count * side), bf16),
-            dma, dma((group,)), dma((group,)), dma((depth,)), dma((depth,)), dma((9,)), dma((9,)),
+            dma, dma((4,)), dma((group,)), dma((group,)), dma((depth,)), dma((depth,)), dma((9,)), dma((9,)),
             dma((steps, group)), dma((steps, group)), dma((steps, depth)), dma((steps, depth)),
             dma((steps, 9)), dma((steps, 9)), dma((steps, 9)), dma((steps, 9)),
         ],
         compiler_params=pltpu.CompilerParams(
-            collective_id=0, has_side_effects=True, vmem_limit_bytes=40 * 2**20
+            collective_id=0, has_side_effects=True, vmem_limit_bytes=60 * 2**20
         ),
         cost_estimate=pl.CostEstimate(flops=10**9, bytes_accessed=4 * 2**20, transcendentals=0),
-    )(tile_columns.reshape(-1), traces, incident, points, coupling.reshape(1, shard), volume_tiles)
+    )(places.reshape(-1), traces, incident, points, coupling.reshape(1, shard), volume_tiles)
     field = field.reshape(tiles_y, tiles_x, excite, side).transpose(2, 0, 1, 3)
     return (present, field)
 

time: 60.8 us -> 57.7 us (0.949)
  local copies, waits for them, and re-layouts: 6.88 us -> 4.1 us
  Pallas kernels: 52.8 us -> 51.9 us
  other arithmetic: 0 us -> 0.72 us
    unnamed x11 -> x1, local copies, waits for them, and re-layouts: 4.96 us -> 1.32 us
    reshape x1, local copies, waits for them, and re-layouts: 1.13 us -> 2.17 us  [per_device(): field = field.reshape(tiles_y, tiles_x, excite, side).transpose(2, 0, 1, 3)]
    pallas_call x1, Pallas kernels: 52.8 us -> 51.9 us  [per_device(): pl.pallas_call(functools.partial(body, n_row, n_col, total, tiles_y, tile...]
    add x0 -> x1, other arithmetic: none -> 0.72 us  [per_device(): places = (ys + tile_columns // 3) * (tiles_x + 2) + xs + tile_columns % 3]
where the time goes in v2:
time: 57.7 us; the launch traced here: 57.3 us
  Pallas kernels  51.9 us (90%)
  local copies, waits for them, and re-layouts  4.1 us (7%)
  other arithmetic  0.72 us (1%)
  between operations  0.64 us (1%)
    pallas_call x1, Pallas kernels, per_device(): pl.pallas_call(functools.partial(body, n_row, n_col, total, tiles_y, tile...  51.9 us
    reshape x1, local copies, waits for them, and re-layouts, per_device(): field = field.reshape(tiles_y, tiles_x, excite, side).transpose(2, 0, 1, 3)  2.17 us
    unnamed x1, local copies, waits for them, and re-layouts  1.32 us

profile of v2, /device:TPU:3, one launch (start us, length us, event | category | flops | bytes accessed | tf_op | source)
XLA Modules:
  0.0 57.3 jit_solution(13020558599421872608)
XLA Ops:
  0.6 0.7 %fusion.1 = s32[4,4,4]{2,1,0:T(4,128)S(1)} fusion(s32[4,4,4]{2,1,0:T(4,128)} %param.11), kind=kLoop, calls=%fused_computation.4 | loop fusion | flops 1024 | bytes 512 | tf_op jit(solution)/shard_map/add | solution.py:344
  1.4 0.6 %reshape.13.columns = s32[64]{0:T(128)} reshape(s32[4,4,4]{2,1,0:T(4,128)S(1)} %fusion.1) | data formatting | bytes 512 | tf_op jit(solution)/shard_map/reshape | solution.py:387
  2.0 51.9 %shard_map.77 = (bf16[64,128]{1,0:T(8,128)(2,1)}, f32[16,64,128]{2,1,0:T(8,128)}) custom-call(s32[64]{0:T(128)} %reshape.13.columns, bf16[64,128]{1,0:T(8,128)(2,1)} %traces.1, bf16[64,128]{1,0:T(8,128)(2,1)} %incident_in.1, f32[3,128]{1,0:T(4,128)} %points_in.1, s32[1,128]{1,0:T(1,128)} %bitcast.7, bf16[4,4,4,128,128]{4,3,2,1,0:T(8,128)(2,1)} %volume.1), custom_call_target="tpu_custom_call" | custom-call | flops 1000000000 | bytes 4194304 | tf_op jit(solution)/shard_map/pallas_call | solution.py:345
  53.8 2.2 %copy.10 = f32[4,4,64,128]{3,1,0,2:T(4,128)} copy(f32[4,4,64,128]{3,2,1,0:T(8,128)} %bitcast.6) | data formatting | bytes 1048576 | tf_op jit(solution)/shard_map/reshape | solution.py:388
  56.0 1.3 %copy.12 = bf16[64,128]{1,0:T(8,128)(2,1)} copy(bf16[64,128]{1,0:T(8,128)(2,1)} %get-tuple-element.8) | data formatting | bytes 32768
